TPU v7x, 512 devices: a whole 4x4x16 slice. The times are simulated.
512 devices in a mesh: tx: 4 (over y), ty: 8 (over x, core), depth: 16 (over z).
Axes of the slice: x: 4, y: 4, z: 16, core: 2. Of those that a mesh axis runs over, the one named last changes fastest.
Arguments:
- volume: bfloat16 [512, 2048, 512], P('depth', 'ty', 'tx'), may hold values from -6 to 6
- transfer: float32 [4, 2], replicated, may hold values from -1.5 to 1.5
- ray_start: int32 [16, 2048, 512], P('depth', 'ty', 'tx'), may hold values from 0 to 15
- ray_stop: int32 [16, 2048, 512], P('depth', 'ty', 'tx'), may hold values from 16 to 32
- pattern: int32 [16, 256, 4], P('depth', 'ty', 'tx'), may hold values 0 or 1
- depth_order: int32 [16], replicated, may hold values from 0 to 15, each once
Outputs:
- frame: float32 [4, 2048, 512], P(None, 'ty', 'tx')
Inputs may be any that keep to these rules, and one draw needn't show every extreme that they name: ray_start[s] < ray_stop[s] for every ray and slice. `depth_order`: each slice appears once.
All inputs are finite; a program needn't handle non-finite values. No bound on the sum of `pattern` on one device may be relied on, other than what follows from the above.
Results may differ from a plain program's by a relative error of at most 0.0003.
Values may be sent and summed in bfloat16 or wider, within the bound.
No kernel may reach another device: no remote copies, remote signals or barrier semaphores. Data moves between devices by JAX's collectives and lax.ppermute only.
A program may use at most 64 MiB of HBM per device.

v0:
```python
import jax
import jax.numpy as jnp
from jax import lax
from jax.sharding import PartitionSpec as P


def extended(array, sides, width):
    edges = {}
    for axis, dim in sides:
        count, length = (lax.axis_size(axis), array.shape[dim])
        up = [(i, (i + 1) % count) for i in range(count - 1)]
        last = lax.slice_in_dim(array, length - width, length, axis=dim)
        initial = lax.slice_in_dim(array, 0, width, axis=dim)
        edges[dim] = (
            lax.ppermute(last, axis, up),
            lax.ppermute(initial, axis, [(b, a) for a, b in up]),
        )
    done = []
    for _, dim in sides:
        low, high = edges[dim]
        around = [(width, width) if d in done else (0, 0) for d in range(array.ndim)]
        array = jnp.concatenate([jnp.pad(low, around), array, jnp.pad(high, around)], axis=dim)
        done.append(dim)
    return array


def local_partial(padded, transfer, ray_start, ray_stop, pattern, depth_count):
    samples = padded.shape[0] - 2
    values = padded[1:-1, 1:-1, 1:-1]
    grad_z = (padded[2:, 1:-1, 1:-1] - padded[:-2, 1:-1, 1:-1]) * 0.5
    grad_y = (padded[1:-1, 2:, 1:-1] - padded[1:-1, :-2, 1:-1]) * 0.5
    grad_x = (padded[1:-1, 1:-1, 2:] - padded[1:-1, 1:-1, :-2]) * 0.5
    lit = jnp.abs(0.48 * grad_x + 0.6 * grad_y + 0.64 * grad_z)
    shading = 0.3 + 0.7 * lit / jnp.sqrt(grad_x * grad_x + grad_y * grad_y + grad_z * grad_z + 1.0)
    rows_each = ray_start.shape[0] // pattern.shape[0]
    cols_each = ray_start.shape[1] // pattern.shape[1]
    pattern_full = jnp.repeat(jnp.repeat(pattern, rows_each, axis=0), cols_each, axis=1)
    layers = lax.broadcasted_iota(jnp.int32, (samples, 1, 1), 0)
    active = (layers >= ray_start[None]) & (layers < ray_stop[None]) & (pattern_full[None] > 0)
    density = jax.nn.softplus(transfer[3, 0] * values + transfer[3, 1]) * (
        2.0 / (samples * depth_count)
    )
    opacity = jnp.where(active, 1.0 - jnp.exp(-density), jnp.float32(0.0))
    passed = jnp.cumprod(1.0 - opacity, axis=0)
    prior = jnp.concatenate([jnp.ones_like(passed[:1]), passed[:-1]], axis=0)
    weights = prior * opacity * shading
    tinted = jax.nn.sigmoid(
        transfer[:3, 0][:, None, None, None] * values[None] + transfer[:3, 1][:, None, None, None]
    )
    colors = jnp.sum(weights[None] * tinted, axis=1)
    return jnp.concatenate([colors, passed[-1][None]], axis=0)


def composite(partials, depth_order):
    count = partials.shape[0]

    def step(position, state_pair):
        colors, remain = state_pair
        slice_part = lax.dynamic_index_in_dim(partials, depth_order[position], 0, keepdims=False)
        return (colors + remain[None] * slice_part[:3], remain * slice_part[3])

    start_pair = (
        jnp.zeros((3,) + partials.shape[2:], jnp.float32),
        jnp.ones(partials.shape[2:], jnp.float32),
    )
    colors, remain = lax.fori_loop(0, count, step, start_pair)
    return jnp.concatenate([colors, 1.0 - remain[None]], axis=0)


def shards(volume, transfer, ray_start, ray_stop, pattern, depth_order):
    padded = extended(volume, (("tx", 2), ("ty", 1), ("depth", 0)), 1).astype(jnp.float32)
    depth_count = lax.axis_size("depth")
    stacked = local_partial(padded, transfer, ray_start[0], ray_stop[0], pattern[0], depth_count)[
        None
    ]
    pixel_share = lax.all_to_all(stacked, "depth", split_axis=2, concat_axis=0, tiled=True)
    picture = composite(pixel_share, depth_order)
    return lax.all_gather(picture, "depth", axis=1, tiled=True)


def solution(mesh):
    in_specs = (
        P("depth", "ty", "tx"),
        P(),
        P("depth", "ty", "tx"),
        P("depth", "ty", "tx"),
        P("depth", "ty", "tx"),
        P(),
    )
    out_specs = P(None, "ty", "tx")
    return jax.shard_map(shards, mesh=mesh, in_specs=in_specs, out_specs=out_specs, check_vma=False)
```

profile of v0, /device:TPU:24, one launch (start us, length us, event | category | flops | bytes accessed | tf_op | source)
XLA Modules:
  0.0 199.9 jit_solution(10582260819200057759)
XLA Ops:
  0.0 0.9 fusion.31
  0.9 1.7 collective-permute-start.1
  2.7 1.3 collective-permute-start.4
  4.0 0.9 fusion.30
  4.8 3.8 %collective-permute-start = (bf16[1,256,128]{2,1,0:T(8,128)(2,1)S(1)}, bf16[1,256,128]{2,1,0:T(8,128)(2,1)S(1)}, u32[]{:S(2)}, u32[]{:S(2)}) collective-permute-start(bf16[1,256,128]{2,1,0:T(8,128)(2,1)S(1)} %get-tuple-element.151), channel_id=1, source_target_pairs={{0,1},{1,2},{2,3},{3,4},{4,5},{5,6},{6,7},{7,8},{8,9},{9,10},{10,1... | collective-permute-start | bytes 196616 | tf_op jit(solution)/shard_map/ppermute | solution.py:15
  8.7 0.0 copy-start.2
  8.7 0.0 copy-start.3
  8.7 1.3 collective-permute-start.5
  10.0 4.4 %fusion.29 = (bf16[32,256,1]{2,1,0:T(8,128)(2,1)}, bf16[32,256,1]{2,1,0:T(8,128)(2,1)S(1)}) fusion(bf16[32,256,128]{2,1,0:T(8,128)(2,1)} %param.8), kind=kLoop, calls=%fused_computation.52 | loop fusion | bytes 65536 | tf_op jit(solution)/shard_map/slice | solution.py:12
  14.4 2.0 copy.23
  16.3 1.3 collective-permute-start.2
  17.6 0.0 copy-done.2
  17.6 0.0 copy-done.3
  17.7 0.9 copy.24
  18.6 3.4 %collective-permute-done.2 = bf16[32,256,1]{1,0,2:T(8,128)(2,1)S(1)} collective-permute-done((bf16[32,256,1]{1,0,2:T(8,128)(2,1)S(1)}, bf16[32,256,1]{1,0,2:T(8,128)(2,1)S(1)}, u32[]{:S(2)}, u32[]{:S(2)}) %collective-permute-start.2) | collective-permute-done | bytes 16416 | tf_op jit(solution)/shard_map/ppermute | solution.py:15
  22.0 2.6 %collective-permute-start.3 = (bf16[32,256,1]{1,0,2:T(8,128)(2,1)S(1)}, bf16[32,256,1]{1,0,2:T(8,128)(2,1)S(1)}, u32[]{:S(2)}, u32[]{:S(2)}) collective-permute-start(bf16[32,256,1]{1,0,2:T(8,128)(2,1)S(1)} %copy.24), channel_id=1, source_target_pairs={{128,0},{256,128},{384,256},{129,1},{257,129},{385,257},{130,2},{2... | collective-permute-start | bytes 49160 | tf_op jit(solution)/shard_map/ppermute | solution.py:16
  24.6 0.7 fusion.32
  25.3 0.1 broadcast_in_dim.24
  25.3 0.1 gt.22
  25.4 1.9 copy.17
  27.3 0.0 collective-permute-done.3
  27.3 1.8 copy.18
  29.2 0.0 copy-start
  29.2 0.0 copy-start.1
  29.2 0.0 collective-permute-done.1
  29.2 0.0 collective-permute-done.4
  29.2 0.0 collective-permute-done
  29.2 0.0 collective-permute-done.5
  29.2 17.7 %fusion.11 = f32[34,258,130]{2,1,0:T(8,128)S(1)} fusion(bf16[1,256,128]{2,1,0:T(8,128)(2,1)S(1)} %collective-permute-done.5, bf16[32,1,128]{2,1,0:T(2,128)(2,1)S(1)} %collective-permute-done.4, bf16[32,1,128]{2,1,0:T(2,128)(2,1)S(1)} %collective-permute-done.1, bf16[1,256,128]{2,1,0:T(8,128)(2,1)S(1)} %collective-permute-done, bf16[32,256,1]{2,1,0:T(8,128)(2,1)} %copy.18, ...), kind=kLoop, calls=%fused_computation.23 | loop fusion | flops 33070440 | bytes 6838816 | tf_op jit(solution)/shard_map/convert_element_type | solution.py:71
  46.9 0.0 copy-done
  46.9 0.0 copy-done.1
  46.9 7.6 %fusion.22 = f32[32,256,128]{2,1,0:T(8,128)} fusion(f32[]{:T(128)} %bitcast.4, f32[]{:T(128)} %bitcast.3, s32[256,128]{1,0:T(8,128)S(1)} %bitcast.41, s32[256,128]{1,0:T(8,128)S(1)} %bitcast.43, pred[256]{0:T(512)(128)(4,1)S(1)} %gt.22, f32[34,258,130]{2,1,0:T(8,128)S(1)} %fusion.11), kind=kOutput, calls=%fused_computation.38 | output fusion | flops 50331648 | bytes 8651272 | tf_op jit(solution)/shard_map/jit(cumprod)/reduce_window | solution.py:44
  54.5 4.5 %slice.100 = f32[31,256,128]{2,1,0:T(8,128)} slice(f32[32,256,128]{2,1,0:T(8,128)} %fusion.22), slice={[0:31], [0:256], [0:128]} | slice | bytes 8126464 | tf_op jit(solution)/shard_map/slice | solution.py:45
  59.0 13.6 %add_multiply_fusion = (f32[32,256,128]{2,1,0:T(8,128)S(1)}, f32[32,256,128]{2,1,0:T(8,128)S(1)}) fusion(f32[34,258,130]{2,1,0:T(8,128)S(1)} %fusion.11, f32[31,256,128]{2,1,0:T(8,128)} %slice.100, f32[]{:T(128)} %bitcast.4, f32[]{:T(128)} %bitcast.3, pred[256]{0:T(512)(128)(4,1)S(1)} %gt.22, s32[256,128]{1,0:T(8,128)S(1)} %bitcast.42, ...), kind=kLoop, calls=%fused_computation.37 | loop fusion | flops 40894464 | bytes 42074376 | tf_op jit(solution)/shard_map/mul | solution.py:46
  72.6 0.0 slice-start
  72.6 3.8 %multiply_reduce_fusion = f32[3,256,128]{2,1,0:T(8,128)S(1)} fusion(f32[3]{0:T(128)S(1)} %get-tuple-element.156, f32[32,256,128]{2,1,0:T(8,128)S(1)} %get-tuple-element.148, f32[3]{0:T(128)S(1)} %get-tuple-element.155, f32[32,256,128]{2,1,0:T(8,128)S(1)} %get-tuple-element.147), kind=kLoop, calls=%fused_computation.9 | loop fusion | flops 21921792 | bytes 8781848 | tf_op jit(solution)/shard_map/reduce_sum | solution.py:50
  76.5 0.0 slice-done
  76.5 0.0 copy-start.4
  76.5 1.1 copy.19
  77.7 17.1 %all-to-all-start = ((f32[1,4,256,128]{3,1,0,2:T(4,128)}), f32[1,4,256,128]{3,1,0,2:T(4,128)S(1)}, u32[]{:S(2)}, u32[]{:S(2)}) async-start(f32[1,4,256,128]{3,1,0,2:T(4,128)} %copy.19), calls=%async_computation | async-start | bytes 1048576 | tf_op jit(solution)/shard_map/all_to_all | solution.py:76
  94.8 29.3 %all-to-all-done = f32[1,4,256,128]{3,1,0,2:T(4,128)S(1)} async-done(((f32[1,4,256,128]{3,1,0,2:T(4,128)}), f32[1,4,256,128]{3,1,0,2:T(4,128)S(1)}, u32[]{:S(2)}, u32[]{:S(2)}) %all-to-all-start) | async-done | bytes 524320 | tf_op jit(solution)/shard_map/all_to_all | solution.py:76
  124.1 0.0 copy-done.4
  124.1 41.5 %while.16 = (s32[]{:T(128)}, f32[3,16,128]{2,1,0:T(8,128)S(1)}, f32[16,128]{1,0:T(8,128)S(1)}, s32[16]{0:T(128)S(1)}, f32[16,4,16,128]{3,2,0,1:T(8,128)S(1)}, /*index=5*/s32[]{:T(128)}, s32[]{:T(128)}, s32[]{:T(128)}) while((s32[]{:T(128)}, f32[3,16,128]{2,1,0:T(8,128)S(1)}, f32[16,128]{1,0:T(8,128)S(1)}, s32[16]{0:T(128)S(1)}, ...), condition=%wide.region_3.4_spmd.clone, body=%wide.region_2.3_spmd.clone.sunk | while | flops 22534 | bytes 180378 | solution.py:66
  124.2 0.6 dynamic_slice.21
  126.8 0.6 dynamic_slice.21
  129.4 0.6 dynamic_slice.21
  131.9 0.6 dynamic_slice.21
  134.5 0.6 dynamic_slice.21
  137.1 0.6 dynamic_slice.21
  139.7 0.6 dynamic_slice.21
  142.3 0.6 dynamic_slice.21
  144.9 0.6 dynamic_slice.21
  147.5 0.6 dynamic_slice.21
  150.1 0.6 dynamic_slice.21
  152.7 0.6 dynamic_slice.21
  155.3 0.6 dynamic_slice.21
  157.9 0.6 dynamic_slice.21
  160.5 0.6 dynamic_slice.21
  163.1 0.6 dynamic_slice.21
  165.7 33.5 %all_gather.3 = f32[4,256,128]{2,1,0:T(8,128)S(1)} all-gather(f32[4,16,128]{2,1,0:T(8,128)S(1)} %pad_maximum_fusion), channel_id=1, replica_groups=mesh['tx'=4,'ty'=8,'depth'=16] {'depth'}, dimensions={1}, use_global_device_ids=true | all-gather | bytes 557056 | tf_op jit(solution)/shard_map/all_gather | solution.py:78
  199.2 0.8 copy.35
  (56 shorter events, 0.5 us)
Async XLA Ops:
  0.9 28.3 %collective-permute-start.1 = (bf16[32,1,128]{2,1,0:T(2,128)(2,1)S(1)}, bf16[32,1,128]{2,1,0:T(2,128)(2,1)S(1)}, u32[]{:S(2)}, u32[]{:S(2)}) collective-permute-start(bf16[32,1,128]{2,1,0:T(2,128)(2,1)S(1)} %get-tuple-element.153), channel_id=1, source_target_pairs={{0,16},{16,32},{32,48},{48,64},{64,80},{80,96},{96,112},{1,17},{17... | collective-permute-start | bytes 24584 | tf_op jit(solution)/shard_map/ppermute | solution.py:15
  2.7 26.5 %collective-permute-start.4 = (bf16[32,1,128]{2,1,0:T(2,128)(2,1)S(1)}, bf16[32,1,128]{2,1,0:T(2,128)(2,1)S(1)}, u32[]{:S(2)}, u32[]{:S(2)}) collective-permute-start(bf16[32,1,128]{2,1,0:T(2,128)(2,1)S(1)} %get-tuple-element.154), channel_id=1, source_target_pairs={{16,0},{32,16},{48,32},{64,48},{80,64},{96,80},{112,96},{17,1},{33... | collective-permute-start | bytes 24584 | tf_op jit(solution)/shard_map/ppermute | solution.py:16
  4.8 24.3 %collective-permute-start = (bf16[1,256,128]{2,1,0:T(8,128)(2,1)S(1)}, bf16[1,256,128]{2,1,0:T(8,128)(2,1)S(1)}, u32[]{:S(2)}, u32[]{:S(2)}) collective-permute-start(bf16[1,256,128]{2,1,0:T(8,128)(2,1)S(1)} %get-tuple-element.151), channel_id=1, source_target_pairs={{0,1},{1,2},{2,3},{3,4},{4,5},{5,6},{6,7},{7,8},{8,9},{9,10},{10,1... | collective-permute-start | bytes 196616 | tf_op jit(solution)/shard_map/ppermute | solution.py:15
  8.7 9.0 %copy-start.2 = (f32[4,2]{0,1:T(2,128)S(1)}, f32[4,2]{0,1:T(2,128)}, u32[]{:S(2)}) copy-start(f32[4,2]{0,1:T(2,128)} %param.9) | copy-start | bytes 100
  8.7 9.0 %copy-start.3 = (s32[1,32,1]{1,2,0:T(1,128)S(1)}, s32[1,32,1]{1,2,0:T(1,128)}, u32[]{:S(2)}) copy-start(s32[1,32,1]{1,2,0:T(1,128)} %param.12) | copy-start | bytes 388
  8.7 20.5 %collective-permute-start.5 = (bf16[1,256,128]{2,1,0:T(8,128)(2,1)S(1)}, bf16[1,256,128]{2,1,0:T(8,128)(2,1)S(1)}, u32[]{:S(2)}, u32[]{:S(2)}) collective-permute-start(bf16[1,256,128]{2,1,0:T(8,128)(2,1)S(1)} %get-tuple-element.152), channel_id=1, source_target_pairs={{1,0},{2,1},{3,2},{4,3},{5,4},{6,5},{7,6},{8,7},{9,8},{10,9},{11,1... | collective-permute-start | bytes 196616 | tf_op jit(solution)/shard_map/ppermute | solution.py:16
  16.3 5.6 %collective-permute-start.2 = (bf16[32,256,1]{1,0,2:T(8,128)(2,1)S(1)}, bf16[32,256,1]{1,0,2:T(8,128)(2,1)S(1)}, u32[]{:S(2)}, u32[]{:S(2)}) collective-permute-start(bf16[32,256,1]{1,0,2:T(8,128)(2,1)S(1)} %copy.23), channel_id=1, source_target_pairs={{0,128},{128,256},{256,384},{1,129},{129,257},{257,385},{2,130},{1... | collective-permute-start | bytes 49160 | tf_op jit(solution)/shard_map/ppermute | solution.py:15
  22.0 5.4 %collective-permute-start.3 = (bf16[32,256,1]{1,0,2:T(8,128)(2,1)S(1)}, bf16[32,256,1]{1,0,2:T(8,128)(2,1)S(1)}, u32[]{:S(2)}, u32[]{:S(2)}) collective-permute-start(bf16[32,256,1]{1,0,2:T(8,128)(2,1)S(1)} %copy.24), channel_id=1, source_target_pairs={{128,0},{256,128},{384,256},{129,1},{257,129},{385,257},{130,2},{2... | collective-permute-start | bytes 49160 | tf_op jit(solution)/shard_map/ppermute | solution.py:16
  29.2 17.7 %copy-start = (s32[1,256,128]{2,1,0:T(8,128)S(1)}, s32[1,256,128]{2,1,0:T(8,128)}, u32[]{:S(2)}) copy-start(s32[1,256,128]{2,1,0:T(8,128)} %param.11) | copy-start | bytes 393220
  29.2 17.7 %copy-start.1 = (s32[1,256,128]{2,1,0:T(8,128)S(1)}, s32[1,256,128]{2,1,0:T(8,128)}, u32[]{:S(2)}) copy-start(s32[1,256,128]{2,1,0:T(8,128)} %param.10) | copy-start | bytes 393220
  72.6 3.8 %slice-start = ((f32[32,256,128]{2,1,0:T(8,128)}), f32[1,256,128]{2,1,0:T(8,128)S(1)}, s32[]{:S(2)}) async-start(f32[32,256,128]{2,1,0:T(8,128)} %fusion.22), calls=%async_computation.1 | async-start | bytes 262144 | tf_op jit(solution)/shard_map/slice | solution.py:51
  76.5 47.7 %copy-start.4 = (s32[16]{0:T(128)S(1)}, s32[16]{0:T(128)}, u32[]{:S(2)}) copy-start(s32[16]{0:T(128)} %param.13) | copy-start | bytes 196
  77.7 46.4 %all-to-all-start = ((f32[1,4,256,128]{3,1,0,2:T(4,128)}), f32[1,4,256,128]{3,1,0,2:T(4,128)S(1)}, u32[]{:S(2)}, u32[]{:S(2)}) async-start(f32[1,4,256,128]{3,1,0,2:T(4,128)} %copy.19), calls=%async_computation | async-start | bytes 1048576 | tf_op jit(solution)/shard_map/all_to_all | solution.py:76
where the time goes:
time: 201 us; the launch traced here: 200 us
  other arithmetic  43 us (21%)
  blocking collectives  33.5 us (17%)
  waiting for transfers between devices  32.7 us (16%)
  loops' own time  31.7 us (16%)
  local copies, waits for them, and re-layouts  29.6 us (15%)
  starting transfers between devices  29.2 us (15%)
    all_gather x1, blocking collectives, shards(): return lax.all_gather(picture, 'depth', axis=1, tiled=True)  33.5 us
    another operation x1, loops' own time, composite(): colors, remain = lax.fori_loop(0, count, step, start_pair)  31.7 us
    all_to_all x1, waiting for transfers between devices, shards(): lax.all_to_all(stacked, 'depth', split_axis=2, concat_axis=0, tiled=True)  29.3 us
    convert_element_type x1, other arithmetic, shards(): extended(volume, (('tx', 2), ('ty', 1), ('depth', 0)), 1)  17.7 us
    all_to_all x1, starting transfers between devices, shards(): lax.all_to_all(stacked, 'depth', split_axis=2, concat_axis=0, tiled=True)  17.1 us
    mul x1, other arithmetic, local_partial(): weights = prior * opacity * shading  13.6 us
    dynamic_slice x16, local copies, waits for them, and re-layouts, step(): depth_order[position]  9.38 us
    another operation x1, other arithmetic, local_partial(): passed = jnp.cumprod(1.0 - opacity, axis=0)  7.63 us
  transfers between devices with their start and end apart: 7, of which 2 were waited for; matrix products, arithmetic and copies ran while one was open for 6% of the time, Pallas kernels for 0%

commit v1 on v0

--- a/solution.py
+++ b/solution.py
@@ -2,6 +2,24 @@
 import jax.numpy as jnp
 from jax import lax
 from jax.sharding import PartitionSpec as P
+
+
+def gather_around(value, axis, dim):
+    ways, here, step = (lax.axis_size(axis), lax.axis_index(axis), value.shape[dim])
+    shape = [n * ways if d == dim else n for d, n in enumerate(value.shape)]
+    full = lax.dynamic_update_slice_in_dim(
+        jnp.zeros(shape, value.dtype), value, here * step, axis=dim
+    )
+    going_up = going_down = value
+    for far in range(1, ways // 2 + 1):
+        going_up = lax.ppermute(going_up, axis, [(d, (d + 1) % ways) for d in range(ways)])
+        full = lax.dynamic_update_slice_in_dim(full, going_up, (here - far) % ways * step, axis=dim)
+        if 2 * far < ways:
+            going_down = lax.ppermute(going_down, axis, [(d, (d - 1) % ways) for d in range(ways)])
+            full = lax.dynamic_update_slice_in_dim(
+                full, going_down, (here + far) % ways * step, axis=dim
+            )
+    return full
 
 
 def extended(array, sides, width):
@@ -75,7 +93,7 @@
     ]
     pixel_share = lax.all_to_all(stacked, "depth", split_axis=2, concat_axis=0, tiled=True)
     picture = composite(pixel_share, depth_order)
-    return lax.all_gather(picture, "depth", axis=1, tiled=True)
+    return gather_around(picture, "depth", 1)
 
 
 def solution(mesh):

time: 201 us -> 227 us (1.13); the launches traced: 200 us -> 223 us
  starting transfers between devices: 29.2 us -> 82.2 us
  blocking collectives: 33.5 us -> 0 us
  waiting for transfers between devices: 32.7 us -> 35.5 us
    ppermute x0 -> x15, starting transfers between devices: none -> 53 us  [the longest x7 35.6 us: gather_around(): lax.ppermute(going_down, axis, [(d, (d - 1) % ways) for d in range(ways)])]
    all_gather x1 -> x0, blocking collectives: 33.5 us -> none  [shards(): return lax.all_gather(picture, 'depth', axis=1, tiled=True)]
    ppermute x0 -> x15, waiting for transfers between devices: none -> 5.21 us  [the longest x8 5.19 us: gather_around(): lax.ppermute(going_up, axis, [(d, (d + 1) % ways) for d in range(ways)])]
  transfers between devices with their start and end apart: 7 -> 22, of which waited for: 2 -> 5; matrix products, arithmetic and copies ran while one was open for 6% -> 6% of each run, Pallas kernels for 0% -> 0%
where the time goes in v1:
time: 227 us; the launch traced here: 223 us
  starting transfers between devices  82.2 us (36%)
  other arithmetic  43 us (19%)
  waiting for transfers between devices  35.5 us (16%)
  loops' own time  31.8 us (14%)
  local copies, waits for them, and re-layouts  29.7 us (13%)
    ppermute x7, starting transfers between devices, gather_around(): lax.ppermute(going_down, axis, [(d, (d - 1) % ways) for d in range(ways)])  35.6 us
    another operation x1, loops' own time, composite(): colors, remain = lax.fori_loop(0, count, step, start_pair)  31.8 us
    all_to_all x1, waiting for transfers between devices, shards(): lax.all_to_all(stacked, 'depth', split_axis=2, concat_axis=0, tiled=True)  27.9 us
    convert_element_type x1, other arithmetic, shards(): extended(volume, (('tx', 2), ('ty', 1), ('depth', 0)), 1)  17.7 us
    ppermute x8, starting transfers between devices, gather_around(): lax.ppermute(going_up, axis, [(d, (d + 1) % ways) for d in range(ways)])  17.4 us
    all_to_all x1, starting transfers between devices, shards(): lax.all_to_all(stacked, 'depth', split_axis=2, concat_axis=0, tiled=True)  15.2 us
    mul x1, other arithmetic, local_partial(): weights = prior * opacity * shading  13.6 us
    dynamic_slice x16, local copies, waits for them, and re-layouts, step(): depth_order[position]  9.38 us
  transfers between devices with their start and end apart: 22, of which 5 were waited for; matrix products, arithmetic and copies ran while one was open for 6% of the time, Pallas kernels for 0%

profile of v1, /device:TPU:24, one launch (start us, length us, event | category | flops | bytes accessed | tf_op | source)
XLA Modules:
  0.0 223.2 jit_solution(13624926779371231949)
XLA Ops:
  0.0 0.9 fusion.30
  0.9 1.3 collective-permute-start.5
  2.2 0.9 fusion.31
  3.1 1.3 collective-permute-start.4
  4.4 3.0 %collective-permute-start.1 = (bf16[32,1,128]{2,1,0:T(2,128)(2,1)S(1)}, bf16[32,1,128]{2,1,0:T(2,128)(2,1)S(1)}, u32[]{:S(2)}, u32[]{:S(2)}) collective-permute-start(bf16[32,1,128]{2,1,0:T(2,128)(2,1)S(1)} %get-tuple-element.153), channel_id=1, source_target_pairs={{0,16},{16,32},{32,48},{48,64},{64,80},{80,96},{96,112},{1,17},{17... | collective-permute-start | bytes 24584 | tf_op jit(solution)/shard_map/ppermute | solution.py:33
  7.4 0.0 copy-start.3
  7.4 0.0 copy-start.4
  7.5 4.5 %collective-permute-start = (bf16[1,256,128]{2,1,0:T(8,128)(2,1)S(1)}, bf16[1,256,128]{2,1,0:T(8,128)(2,1)S(1)}, u32[]{:S(2)}, u32[]{:S(2)}) collective-permute-start(bf16[1,256,128]{2,1,0:T(8,128)(2,1)S(1)} %get-tuple-element.151), channel_id=1, source_target_pairs={{0,1},{1,2},{2,3},{3,4},{4,5},{5,6},{6,7},{7,8},{8,9},{9,10},{10,1... | collective-permute-start | bytes 196616 | tf_op jit(solution)/shard_map/ppermute | solution.py:33
  12.0 4.5 %fusion.29 = (bf16[32,256,1]{2,1,0:T(8,128)(2,1)S(1)}, bf16[32,256,1]{2,1,0:T(8,128)(2,1)}) fusion(bf16[32,256,128]{2,1,0:T(8,128)(2,1)} %param.8), kind=kLoop, calls=%fused_computation.68 | loop fusion | bytes 65536 | tf_op jit(solution)/shard_map/slice | solution.py:30
  16.5 2.0 copy.24
  18.4 2.6 %collective-permute-start.3 = (bf16[32,256,1]{1,0,2:T(8,128)(2,1)S(1)}, bf16[32,256,1]{1,0,2:T(8,128)(2,1)S(1)}, u32[]{:S(2)}, u32[]{:S(2)}) collective-permute-start(bf16[32,256,1]{1,0,2:T(8,128)(2,1)S(1)} %copy.24), channel_id=1, source_target_pairs={{128,0},{256,128},{384,256},{129,1},{257,129},{385,257},{130,2},{2... | collective-permute-start | bytes 49160 | tf_op jit(solution)/shard_map/ppermute | solution.py:34
  21.1 0.9 copy.23
  22.0 0.5 collective-permute-done.3
  22.5 1.3 collective-permute-start.2
  23.8 0.7 fusion.32
  24.5 0.1 broadcast_in_dim.28
  24.6 0.1 gt.22
  24.6 1.8 copy.18
  26.5 2.0 collective-permute-done.2
  28.5 1.8 copy.17
  30.3 17.7 %fusion.11 = f32[34,258,130]{2,1,0:T(8,128)S(1)} fusion(bf16[1,256,128]{2,1,0:T(8,128)(2,1)S(1)} %collective-permute-done.5, bf16[32,1,128]{2,1,0:T(2,128)(2,1)S(1)} %collective-permute-done.4, bf16[32,1,128]{2,1,0:T(2,128)(2,1)S(1)} %collective-permute-done.1, bf16[1,256,128]{2,1,0:T(8,128)(2,1)S(1)} %collective-permute-done, bf16[32,256,1]{2,1,0:T(8,128)(2,1)} %copy.18, ...), kind=kLoop, calls=%fused_computation.23 | loop fusion | flops 33070440 | bytes 6838816 | tf_op jit(solution)/shard_map/convert_element_type | solution.py:89
  48.0 7.7 %fusion.22 = f32[32,256,128]{2,1,0:T(8,128)} fusion(f32[]{:T(128)} %bitcast.4, f32[]{:T(128)} %bitcast.3, s32[256,128]{1,0:T(8,128)S(1)} %bitcast.41, s32[256,128]{1,0:T(8,128)S(1)} %bitcast.43, pred[256]{0:T(512)(128)(4,1)S(1)} %gt.22, f32[34,258,130]{2,1,0:T(8,128)S(1)} %fusion.11), kind=kOutput, calls=%fused_computation.38 | output fusion | flops 50331648 | bytes 8651272 | tf_op jit(solution)/shard_map/jit(cumprod)/reduce_window | solution.py:62
  55.7 4.6 %slice.100 = f32[31,256,128]{2,1,0:T(8,128)} slice(f32[32,256,128]{2,1,0:T(8,128)} %fusion.22), slice={[0:31], [0:256], [0:128]} | slice | bytes 8126464 | tf_op jit(solution)/shard_map/slice | solution.py:63
  60.2 13.6 %add_multiply_fusion = (f32[32,256,128]{2,1,0:T(8,128)S(1)}, f32[32,256,128]{2,1,0:T(8,128)S(1)}) fusion(f32[34,258,130]{2,1,0:T(8,128)S(1)} %fusion.11, f32[31,256,128]{2,1,0:T(8,128)} %slice.100, f32[]{:T(128)} %bitcast.4, f32[]{:T(128)} %bitcast.3, pred[256]{0:T(512)(128)(4,1)S(1)} %gt.22, s32[256,128]{1,0:T(8,128)S(1)} %bitcast.42, ...), kind=kLoop, calls=%fused_computation.37 | loop fusion | flops 40894464 | bytes 42074376 | tf_op jit(solution)/shard_map/mul | solution.py:64
  73.8 3.8 %multiply_reduce_fusion = f32[3,256,128]{2,1,0:T(8,128)S(1)} fusion(f32[3]{0:T(128)S(1)} %get-tuple-element.158, f32[32,256,128]{2,1,0:T(8,128)S(1)} %get-tuple-element.148, f32[3]{0:T(128)S(1)} %get-tuple-element.157, f32[32,256,128]{2,1,0:T(8,128)S(1)} %get-tuple-element.147), kind=kLoop, calls=%fused_computation.9 | loop fusion | flops 21921792 | bytes 8781848 | tf_op jit(solution)/shard_map/reduce_sum | solution.py:68
  77.7 1.1 copy.19
  78.9 15.2 %all-to-all-start = ((f32[1,4,256,128]{3,1,0,2:T(4,128)}), f32[1,4,256,128]{3,1,0,2:T(4,128)S(1)}, u32[]{:S(2)}, u32[]{:S(2)}) async-start(f32[1,4,256,128]{3,1,0,2:T(4,128)} %copy.19), calls=%async_computation | async-start | bytes 1048576 | tf_op jit(solution)/shard_map/all_to_all | solution.py:94
  94.1 27.9 %all-to-all-done = f32[1,4,256,128]{3,1,0,2:T(4,128)S(1)} async-done(((f32[1,4,256,128]{3,1,0,2:T(4,128)}), f32[1,4,256,128]{3,1,0,2:T(4,128)S(1)}, u32[]{:S(2)}, u32[]{:S(2)}) %all-to-all-start) | async-done | bytes 524320 | tf_op jit(solution)/shard_map/all_to_all | solution.py:94
  122.0 41.5 %while.16 = (s32[]{:T(128)}, f32[3,16,128]{2,1,0:T(8,128)S(1)}, f32[16,128]{1,0:T(8,128)S(1)}, s32[16]{0:T(128)S(1)}, f32[16,4,16,128]{3,2,0,1:T(8,128)S(1)}, /*index=5*/s32[]{:T(128)}, s32[]{:T(128)}, s32[]{:T(128)}) while((s32[]{:T(128)}, f32[3,16,128]{2,1,0:T(8,128)S(1)}, f32[16,128]{1,0:T(8,128)S(1)}, s32[16]{0:T(128)S(1)}, ...), condition=%wide.region_3.4_spmd.clone, body=%wide.region_2.3_spmd.clone.sunk | while | flops 22534 | bytes 180378 | solution.py:84
  122.0 0.6 dynamic_slice.21
  124.6 0.6 dynamic_slice.21
  127.2 0.6 dynamic_slice.21
  129.8 0.6 dynamic_slice.21
  132.4 0.6 dynamic_slice.21
  135.0 0.6 dynamic_slice.21
  137.6 0.6 dynamic_slice.21
  140.2 0.6 dynamic_slice.21
  142.8 0.6 dynamic_slice.21
  145.4 0.6 dynamic_slice.21
  148.0 0.6 dynamic_slice.21
  150.6 0.6 dynamic_slice.21
  153.2 0.6 dynamic_slice.21
  155.8 0.6 dynamic_slice.21
  158.4 0.6 dynamic_slice.21
  161.0 0.6 dynamic_slice.21
  163.6 3.9 %collective-permute-start.6 = (f32[4,16,128]{2,1,0:T(8,128)S(1)}, f32[4,16,128]{2,1,0:T(8,128)S(1)}, u32[]{:S(2)}, u32[]{:S(2)}) collective-permute-start(f32[4,16,128]{2,1,0:T(8,128)S(1)} %get-tuple-element.155), channel_id=1, source_target_pairs={{0,1},{1,2},{2,3},{3,4},{4,5},{5,6},{6,7},{7,8},{8,9},{9,10},{10,1... | collective-permute-start | bytes 98312 | tf_op jit(solution)/shard_map/ppermute | solution.py:15
  167.6 4.8 %collective-permute-start.7 = (f32[4,16,128]{2,1,0:T(8,128)S(1)}, f32[4,16,128]{2,1,0:T(8,128)S(1)}, u32[]{:S(2)}, u32[]{:S(2)}) collective-permute-start(f32[4,16,128]{2,1,0:T(8,128)S(1)} %get-tuple-element.155), channel_id=1, source_target_pairs={{0,15},{1,0},{2,1},{3,2},{4,3},{5,4},{6,5},{7,6},{8,7},{9,8},{10,9... | collective-permute-start | bytes 98312 | tf_op jit(solution)/shard_map/ppermute | solution.py:18
  172.6 1.9 collective-permute-start.8
  174.6 5.1 %collective-permute-start.9 = (f32[4,16,128]{2,1,0:T(8,128)S(1)}, f32[4,16,128]{2,1,0:T(8,128)S(1)}, u32[]{:S(2)}, u32[]{:S(2)}) collective-permute-start(f32[4,16,128]{2,1,0:T(8,128)S(1)} %collective-permute-done.7), channel_id=1, source_target_pairs={{0,15},{1,0},{2,1},{3,2},{4,3},{5,4},{6,5},{7,6},{8,7},{9,8},{10,9... | collective-permute-start | bytes 98312 | tf_op jit(solution)/shard_map/ppermute | solution.py:18
  179.8 1.9 collective-permute-start.10
  181.7 5.2 %collective-permute-start.11 = (f32[4,16,128]{2,1,0:T(8,128)S(1)}, f32[4,16,128]{2,1,0:T(8,128)S(1)}, u32[]{:S(2)}, u32[]{:S(2)}) collective-permute-start(f32[4,16,128]{2,1,0:T(8,128)S(1)} %collective-permute-done.9), channel_id=1, source_target_pairs={{0,15},{1,0},{2,1},{3,2},{4,3},{5,4},{6,5},{7,6},{8,7},{9,8},{10,9... | collective-permute-start | bytes 98312 | tf_op jit(solution)/shard_map/ppermute | solution.py:18
  186.9 0.1 collective-permute-done.10
  187.1 1.9 collective-permute-start.12
  189.0 5.1 %collective-permute-start.13 = (f32[4,16,128]{2,1,0:T(8,128)S(1)}, f32[4,16,128]{2,1,0:T(8,128)S(1)}, u32[]{:S(2)}, u32[]{:S(2)}) collective-permute-start(f32[4,16,128]{2,1,0:T(8,128)S(1)} %collective-permute-done.11), channel_id=1, source_target_pairs={{0,15},{1,0},{2,1},{3,2},{4,3},{5,4},{6,5},{7,6},{8,7},{9,8},{10,9... | collective-permute-start | bytes 98312 | tf_op jit(solution)/shard_map/ppermute | solution.py:18
  194.2 1.9 collective-permute-start.14
  196.1 5.1 %collective-permute-start.15 = (f32[4,16,128]{2,1,0:T(8,128)S(1)}, f32[4,16,128]{2,1,0:T(8,128)S(1)}, u32[]{:S(2)}, u32[]{:S(2)}) collective-permute-start(f32[4,16,128]{2,1,0:T(8,128)S(1)} %collective-permute-done.13), channel_id=1, source_target_pairs={{0,15},{1,0},{2,1},{3,2},{4,3},{5,4},{6,5},{7,6},{8,7},{9,8},{10,9... | collective-permute-start | bytes 98312 | tf_op jit(solution)/shard_map/ppermute | solution.py:18
  201.3 1.9 collective-permute-start.16
  203.2 5.1 %collective-permute-start.17 = (f32[4,16,128]{2,1,0:T(8,128)S(1)}, f32[4,16,128]{2,1,0:T(8,128)S(1)}, u32[]{:S(2)}, u32[]{:S(2)}) collective-permute-start(f32[4,16,128]{2,1,0:T(8,128)S(1)} %collective-permute-done.15), channel_id=1, source_target_pairs={{0,15},{1,0},{2,1},{3,2},{4,3},{5,4},{6,5},{7,6},{8,7},{9,8},{10,9... | collective-permute-start | bytes 98312 | tf_op jit(solution)/shard_map/ppermute | solution.py:18
  208.4 1.9 collective-permute-start.18
  210.4 5.1 %collective-permute-start.19 = (f32[4,16,128]{2,1,0:T(8,128)S(1)}, f32[4,16,128]{2,1,0:T(8,128)S(1)}, u32[]{:S(2)}, u32[]{:S(2)}) collective-permute-start(f32[4,16,128]{2,1,0:T(8,128)S(1)} %collective-permute-done.17), channel_id=1, source_target_pairs={{0,15},{1,0},{2,1},{3,2},{4,3},{5,4},{6,5},{7,6},{8,7},{9,8},{10,9... | collective-permute-start | bytes 98312 | tf_op jit(solution)/shard_map/ppermute | solution.py:18
  215.5 1.9 collective-permute-start.20
  217.5 0.0 copy-start.2
  217.5 5.0 %collective-permute-done.20 = f32[4,16,128]{2,1,0:T(8,128)S(1)} collective-permute-done((f32[4,16,128]{2,1,0:T(8,128)S(1)}, f32[4,16,128]{2,1,0:T(8,128)S(1)}, u32[]{:S(2)}, u32[]{:S(2)}) %collective-permute-start.20) | collective-permute-done | bytes 32800 | tf_op jit(solution)/shard_map/ppermute | solution.py:15
  222.6 0.6 constant_dynamic-update-slice_fusion
  (99 shorter events, 0.7 us)
Async XLA Ops:
  0.9 29.4 %collective-permute-start.5 = (bf16[1,256,128]{2,1,0:T(8,128)(2,1)S(1)}, bf16[1,256,128]{2,1,0:T(8,128)(2,1)S(1)}, u32[]{:S(2)}, u32[]{:S(2)}) collective-permute-start(bf16[1,256,128]{2,1,0:T(8,128)(2,1)S(1)} %get-tuple-element.152), channel_id=1, source_target_pairs={{1,0},{2,1},{3,2},{4,3},{5,4},{6,5},{7,6},{8,7},{9,8},{10,9},{11,1... | collective-permute-start | bytes 196616 | tf_op jit(solution)/shard_map/ppermute | solution.py:34
  3.1 27.2 %collective-permute-start.4 = (bf16[32,1,128]{2,1,0:T(2,128)(2,1)S(1)}, bf16[32,1,128]{2,1,0:T(2,128)(2,1)S(1)}, u32[]{:S(2)}, u32[]{:S(2)}) collective-permute-start(bf16[32,1,128]{2,1,0:T(2,128)(2,1)S(1)} %get-tuple-element.154), channel_id=1, source_target_pairs={{16,0},{32,16},{48,32},{64,48},{80,64},{96,80},{112,96},{17,1},{33... | collective-permute-start | bytes 24584 | tf_op jit(solution)/shard_map/ppermute | solution.py:34
  4.4 25.9 %collective-permute-start.1 = (bf16[32,1,128]{2,1,0:T(2,128)(2,1)S(1)}, bf16[32,1,128]{2,1,0:T(2,128)(2,1)S(1)}, u32[]{:S(2)}, u32[]{:S(2)}) collective-permute-start(bf16[32,1,128]{2,1,0:T(2,128)(2,1)S(1)} %get-tuple-element.153), channel_id=1, source_target_pairs={{0,16},{16,32},{32,48},{48,64},{64,80},{80,96},{96,112},{1,17},{17... | collective-permute-start | bytes 24584 | tf_op jit(solution)/shard_map/ppermute | solution.py:33
  7.4 13.7 %copy-start.3 = (f32[4,2]{0,1:T(2,128)S(1)}, f32[4,2]{0,1:T(2,128)}, u32[]{:S(2)}) copy-start(f32[4,2]{0,1:T(2,128)} %param.9) | copy-start | bytes 100
  7.4 13.7 %copy-start.4 = (s32[1,32,1]{1,2,0:T(1,128)S(1)}, s32[1,32,1]{1,2,0:T(1,128)}, u32[]{:S(2)}) copy-start(s32[1,32,1]{1,2,0:T(1,128)} %param.12) | copy-start | bytes 388
  7.5 22.9 %collective-permute-start = (bf16[1,256,128]{2,1,0:T(8,128)(2,1)S(1)}, bf16[1,256,128]{2,1,0:T(8,128)(2,1)S(1)}, u32[]{:S(2)}, u32[]{:S(2)}) collective-permute-start(bf16[1,256,128]{2,1,0:T(8,128)(2,1)S(1)} %get-tuple-element.151), channel_id=1, source_target_pairs={{0,1},{1,2},{2,3},{3,4},{4,5},{5,6},{6,7},{7,8},{8,9},{9,10},{10,1... | collective-permute-start | bytes 196616 | tf_op jit(solution)/shard_map/ppermute | solution.py:33
  18.4 4.1 %collective-permute-start.3 = (bf16[32,256,1]{1,0,2:T(8,128)(2,1)S(1)}, bf16[32,256,1]{1,0,2:T(8,128)(2,1)S(1)}, u32[]{:S(2)}, u32[]{:S(2)}) collective-permute-start(bf16[32,256,1]{1,0,2:T(8,128)(2,1)S(1)} %copy.24), channel_id=1, source_target_pairs={{128,0},{256,128},{384,256},{129,1},{257,129},{385,257},{130,2},{2... | collective-permute-start | bytes 49160 | tf_op jit(solution)/shard_map/ppermute | solution.py:34
  22.5 5.9 %collective-permute-start.2 = (bf16[32,256,1]{1,0,2:T(8,128)(2,1)S(1)}, bf16[32,256,1]{1,0,2:T(8,128)(2,1)S(1)}, u32[]{:S(2)}, u32[]{:S(2)}) collective-permute-start(bf16[32,256,1]{1,0,2:T(8,128)(2,1)S(1)} %copy.23), channel_id=1, source_target_pairs={{0,128},{128,256},{256,384},{1,129},{129,257},{257,385},{2,130},{1... | collective-permute-start | bytes 49160 | tf_op jit(solution)/shard_map/ppermute | solution.py:33
  30.3 17.7 %copy-start = (s32[1,256,128]{2,1,0:T(8,128)S(1)}, s32[1,256,128]{2,1,0:T(8,128)}, u32[]{:S(2)}) copy-start(s32[1,256,128]{2,1,0:T(8,128)} %param.11) | copy-start | bytes 393220
  30.3 17.7 %copy-start.1 = (s32[1,256,128]{2,1,0:T(8,128)S(1)}, s32[1,256,128]{2,1,0:T(8,128)}, u32[]{:S(2)}) copy-start(s32[1,256,128]{2,1,0:T(8,128)} %param.10) | copy-start | bytes 393220
  73.8 3.8 %slice-start = ((f32[32,256,128]{2,1,0:T(8,128)}), f32[1,256,128]{2,1,0:T(8,128)S(1)}, s32[]{:S(2)}) async-start(f32[32,256,128]{2,1,0:T(8,128)} %fusion.22), calls=%async_computation.1 | async-start | bytes 262144 | tf_op jit(solution)/shard_map/slice | solution.py:69
  77.7 44.3 %copy-start.5 = (s32[16]{0:T(128)S(1)}, s32[16]{0:T(128)}, u32[]{:S(2)}) copy-start(s32[16]{0:T(128)} %param.13) | copy-start | bytes 196
  78.9 43.1 %all-to-all-start = ((f32[1,4,256,128]{3,1,0,2:T(4,128)}), f32[1,4,256,128]{3,1,0,2:T(4,128)S(1)}, u32[]{:S(2)}, u32[]{:S(2)}) async-start(f32[1,4,256,128]{3,1,0,2:T(4,128)} %copy.19), calls=%async_computation | async-start | bytes 1048576 | tf_op jit(solution)/shard_map/all_to_all | solution.py:94
  163.6 9.0 %collective-permute-start.6 = (f32[4,16,128]{2,1,0:T(8,128)S(1)}, f32[4,16,128]{2,1,0:T(8,128)S(1)}, u32[]{:S(2)}, u32[]{:S(2)}) collective-permute-start(f32[4,16,128]{2,1,0:T(8,128)S(1)} %get-tuple-element.155), channel_id=1, source_target_pairs={{0,1},{1,2},{2,3},{3,4},{4,5},{5,6},{6,7},{7,8},{8,9},{9,10},{10,1... | collective-permute-start | bytes 98312 | tf_op jit(solution)/shard_map/ppermute | solution.py:15
  167.6 7.0 %collective-permute-start.7 = (f32[4,16,128]{2,1,0:T(8,128)S(1)}, f32[4,16,128]{2,1,0:T(8,128)S(1)}, u32[]{:S(2)}, u32[]{:S(2)}) collective-permute-start(f32[4,16,128]{2,1,0:T(8,128)S(1)} %get-tuple-element.155), channel_id=1, source_target_pairs={{0,15},{1,0},{2,1},{3,2},{4,3},{5,4},{6,5},{7,6},{8,7},{9,8},{10,9... | collective-permute-start | bytes 98312 | tf_op jit(solution)/shard_map/ppermute | solution.py:18
  172.6 7.1 %collective-permute-start.8 = (f32[4,16,128]{2,1,0:T(8,128)S(1)}, f32[4,16,128]{2,1,0:T(8,128)S(1)}, u32[]{:S(2)}, u32[]{:S(2)}) collective-permute-start(f32[4,16,128]{2,1,0:T(8,128)S(1)} %collective-permute-done.6), channel_id=1, source_target_pairs={{0,1},{1,2},{2,3},{3,4},{4,5},{5,6},{6,7},{7,8},{8,9},{9,10},{10,1... | collective-permute-start | bytes 98312 | tf_op jit(solution)/shard_map/ppermute | solution.py:15
  174.6 7.1 %collective-permute-start.9 = (f32[4,16,128]{2,1,0:T(8,128)S(1)}, f32[4,16,128]{2,1,0:T(8,128)S(1)}, u32[]{:S(2)}, u32[]{:S(2)}) collective-permute-start(f32[4,16,128]{2,1,0:T(8,128)S(1)} %collective-permute-done.7), channel_id=1, source_target_pairs={{0,15},{1,0},{2,1},{3,2},{4,3},{5,4},{6,5},{7,6},{8,7},{9,8},{10,9... | collective-permute-start | bytes 98312 | tf_op jit(solution)/shard_map/ppermute | solution.py:18
  179.8 7.3 %collective-permute-start.10 = (f32[4,16,128]{2,1,0:T(8,128)S(1)}, f32[4,16,128]{2,1,0:T(8,128)S(1)}, u32[]{:S(2)}, u32[]{:S(2)}) collective-permute-start(f32[4,16,128]{2,1,0:T(8,128)S(1)} %collective-permute-done.8), channel_id=1, source_target_pairs={{0,1},{1,2},{2,3},{3,4},{4,5},{5,6},{6,7},{7,8},{8,9},{9,10},{10,1... | collective-permute-start | bytes 98312 | tf_op jit(solution)/shard_map/ppermute | solution.py:15
  181.7 7.3 %collective-permute-start.11 = (f32[4,16,128]{2,1,0:T(8,128)S(1)}, f32[4,16,128]{2,1,0:T(8,128)S(1)}, u32[]{:S(2)}, u32[]{:S(2)}) collective-permute-start(f32[4,16,128]{2,1,0:T(8,128)S(1)} %collective-permute-done.9), channel_id=1, source_target_pairs={{0,15},{1,0},{2,1},{3,2},{4,3},{5,4},{6,5},{7,6},{8,7},{9,8},{10,9... | collective-permute-start | bytes 98312 | tf_op jit(solution)/shard_map/ppermute | solution.py:18
  187.1 7.1 %collective-permute-start.12 = (f32[4,16,128]{2,1,0:T(8,128)S(1)}, f32[4,16,128]{2,1,0:T(8,128)S(1)}, u32[]{:S(2)}, u32[]{:S(2)}) collective-permute-start(f32[4,16,128]{2,1,0:T(8,128)S(1)} %collective-permute-done.10), channel_id=1, source_target_pairs={{0,1},{1,2},{2,3},{3,4},{4,5},{5,6},{6,7},{7,8},{8,9},{9,10},{10,1... | collective-permute-start | bytes 98312 | tf_op jit(solution)/shard_map/ppermute | solution.py:15
  189.0 7.1 %collective-permute-start.13 = (f32[4,16,128]{2,1,0:T(8,128)S(1)}, f32[4,16,128]{2,1,0:T(8,128)S(1)}, u32[]{:S(2)}, u32[]{:S(2)}) collective-permute-start(f32[4,16,128]{2,1,0:T(8,128)S(1)} %collective-permute-done.11), channel_id=1, source_target_pairs={{0,15},{1,0},{2,1},{3,2},{4,3},{5,4},{6,5},{7,6},{8,7},{9,8},{10,9... | collective-permute-start | bytes 98312 | tf_op jit(solution)/shard_map/ppermute | solution.py:18
  194.2 7.1 %collective-permute-start.14 = (f32[4,16,128]{2,1,0:T(8,128)S(1)}, f32[4,16,128]{2,1,0:T(8,128)S(1)}, u32[]{:S(2)}, u32[]{:S(2)}) collective-permute-start(f32[4,16,128]{2,1,0:T(8,128)S(1)} %collective-permute-done.12), channel_id=1, source_target_pairs={{0,1},{1,2},{2,3},{3,4},{4,5},{5,6},{6,7},{7,8},{8,9},{9,10},{10,1... | collective-permute-start | bytes 98312 | tf_op jit(solution)/shard_map/ppermute | solution.py:15
  196.1 7.1 %collective-permute-start.15 = (f32[4,16,128]{2,1,0:T(8,128)S(1)}, f32[4,16,128]{2,1,0:T(8,128)S(1)}, u32[]{:S(2)}, u32[]{:S(2)}) collective-permute-start(f32[4,16,128]{2,1,0:T(8,128)S(1)} %collective-permute-done.13), channel_id=1, source_target_pairs={{0,15},{1,0},{2,1},{3,2},{4,3},{5,4},{6,5},{7,6},{8,7},{9,8},{10,9... | collective-permute-start | bytes 98312 | tf_op jit(solution)/shard_map/ppermute | solution.py:18
  201.3 7.1 %collective-permute-start.16 = (f32[4,16,128]{2,1,0:T(8,128)S(1)}, f32[4,16,128]{2,1,0:T(8,128)S(1)}, u32[]{:S(2)}, u32[]{:S(2)}) collective-permute-start(f32[4,16,128]{2,1,0:T(8,128)S(1)} %collective-permute-done.14), channel_id=1, source_target_pairs={{0,1},{1,2},{2,3},{3,4},{4,5},{5,6},{6,7},{7,8},{8,9},{9,10},{10,1... | collective-permute-start | bytes 98312 | tf_op jit(solution)/shard_map/ppermute | solution.py:15
  203.2 7.1 %collective-permute-start.17 = (f32[4,16,128]{2,1,0:T(8,128)S(1)}, f32[4,16,128]{2,1,0:T(8,128)S(1)}, u32[]{:S(2)}, u32[]{:S(2)}) collective-permute-start(f32[4,16,128]{2,1,0:T(8,128)S(1)} %collective-permute-done.15), channel_id=1, source_target_pairs={{0,15},{1,0},{2,1},{3,2},{4,3},{5,4},{6,5},{7,6},{8,7},{9,8},{10,9... | collective-permute-start | bytes 98312 | tf_op jit(solution)/shard_map/ppermute | solution.py:18
  208.4 7.1 %collective-permute-start.18 = (f32[4,16,128]{2,1,0:T(8,128)S(1)}, f32[4,16,128]{2,1,0:T(8,128)S(1)}, u32[]{:S(2)}, u32[]{:S(2)}) collective-permute-start(f32[4,16,128]{2,1,0:T(8,128)S(1)} %collective-permute-done.16), channel_id=1, source_target_pairs={{0,1},{1,2},{2,3},{3,4},{4,5},{5,6},{6,7},{7,8},{8,9},{9,10},{10,1... | collective-permute-start | bytes 98312 | tf_op jit(solution)/shard_map/ppermute | solution.py:15
  210.4 7.1 %collective-permute-start.19 = (f32[4,16,128]{2,1,0:T(8,128)S(1)}, f32[4,16,128]{2,1,0:T(8,128)S(1)}, u32[]{:S(2)}, u32[]{:S(2)}) collective-permute-start(f32[4,16,128]{2,1,0:T(8,128)S(1)} %collective-permute-done.17), channel_id=1, source_target_pairs={{0,15},{1,0},{2,1},{3,2},{4,3},{5,4},{6,5},{7,6},{8,7},{9,8},{10,9... | collective-permute-start | bytes 98312 | tf_op jit(solution)/shard_map/ppermute | solution.py:18
  215.5 7.0 %collective-permute-start.20 = (f32[4,16,128]{2,1,0:T(8,128)S(1)}, f32[4,16,128]{2,1,0:T(8,128)S(1)}, u32[]{:S(2)}, u32[]{:S(2)}) collective-permute-start(f32[4,16,128]{2,1,0:T(8,128)S(1)} %collective-permute-done.18), channel_id=1, source_target_pairs={{0,1},{1,2},{2,3},{3,4},{4,5},{5,6},{6,7},{7,8},{8,9},{9,10},{10,1... | collective-permute-start | bytes 98312 | tf_op jit(solution)/shard_map/ppermute | solution.py:15
  217.5 5.0 %copy-start.2 = (f32[4,256,128]{2,1,0:T(8,128)}, f32[4,256,128]{2,1,0:T(8,128)S(1)}, u32[]{:S(2)}) copy-start(f32[4,256,128]{2,1,0:T(8,128)S(1)} %constant_dynamic-update-slice_fusion.1) | copy-start | bytes 1572868
